TPU v7x, 128 devices: a whole 4x4x4 slice. The times are simulated.
128 devices in a mesh: blk: 16 (over z_hi, x, core), order: 8 (over z_lo, y).
Axes of the slice: x: 4, y: 4, z: 4 (z_hi: 2, z_lo: 2; z = z_hi * 2 + z_lo), core: 2. Of those that a mesh axis runs over, the one named last changes fastest.
Arguments:
- fourier: bfloat16 [16, 128, 32768], P(None, None, ('blk', 'order')), may hold values from -6 to 6
- cycle_lat: int32 [32768], replicated, may hold values from 0 to 32767, as said below
- order_table: int32 [128], replicated, may hold values from 0 to 127, each once
- leaf_op: bfloat16 [128, 128, 32768], P('order', None, 'blk'), may hold values from -0.125 to 0.125
- level_op: bfloat16 [4, 16, 128, 128, 256], P(None, 'blk', 'order'), may hold values from -0.25 to 0.25
- skeleton: int32 [4, 16, 128, 128], P(None, 'blk', 'order'), may hold values from 0 to 255, as said below
- top_op: bfloat16 [128, 16384, 128], P('order', 'blk'), may hold values from -0.5 to 0.5
Outputs:
- alm: float32 [16, 128, 16384], P(None, 'order', 'blk')
Inputs may be any that keep to these rules, and one draw needn't show every extreme that they name: `cycle_lat`: a permutation of the cycles; the 256 stored cycles of each device hold exactly 16 cycles of each leaf block. `skeleton`: each list holds 128 distinct entries.
All inputs are finite; a program needn't handle non-finite values.
Results may differ from a plain program's by a relative error of at most 0.0065.
Values may be sent and summed in bfloat16 or wider, within the bound.
A program may use at most 128 MiB of HBM per device.

v0:
```python
import jax
import jax.numpy as jnp
from jax import lax
from jax.sharding import PartitionSpec as P


def swapped(block, axis, apart):
    count = lax.axis_size(axis)
    route = []
    for low in range(count):
        high = low | 1 << apart
        if high != low and high < count:
            route += [(low, high), (high, low)]
    return lax.ppermute(block, axis, route)


def climb(field_part, leaf_part, mixing_part, chosen_part, level_count):
    coeff = jnp.einsum(
        "jkr,rcj->jck", leaf_part, field_part, preferred_element_type=jnp.float32
    ).astype(jnp.bfloat16)
    width = 2 * coeff.shape[2]
    positions = jnp.arange(width, dtype=jnp.int32)
    for level in range(level_count):
        partner = swapped(coeff, "blk", level)
        combined = jnp.concatenate([coeff, partner], axis=2)
        selector = (chosen_part[level][:, :, None] == positions[None, None, :]).astype(jnp.bfloat16)
        picked = jnp.einsum("jkq,jcq->jck", selector, combined, preferred_element_type=jnp.float32)
        product = jnp.einsum(
            "jkq,jcq->jck", mixing_part[level], combined, preferred_element_type=jnp.float32
        )
        coeff = (picked + product).astype(jnp.bfloat16)
    return coeff


def per_device(fourier, cycle_lat, order_table, leaf_op, level_op, skeleton, top_op):
    blocks = lax.axis_size("blk")
    owners = lax.axis_size("order")
    here_blk = lax.axis_index("blk")
    here_own = lax.axis_index("order")
    cols, orders, rows = fourier.shape
    slots = orders // owners
    cycle_total = cycle_lat.shape[0]
    block_cycles = cycle_total // blocks
    per_block = rows // blocks
    devices = blocks * owners
    level_count = blocks.bit_length() - 1
    table = cycle_lat.reshape(devices, rows)
    block_of = table // block_cycles
    row_ids = jnp.arange(rows, dtype=jnp.int32)
    earlier = row_ids[None, :] < row_ids[:, None]
    within = jnp.sum(
        ((block_of[:, :, None] == block_of[:, None, :]) & earlier[None]).astype(jnp.int32), axis=2
    )
    mine = here_blk * owners + here_own
    own_block = lax.dynamic_index_in_dim(block_of, mine, 0, keepdims=False)
    own_within = lax.dynamic_index_in_dim(within, mine, 0, keepdims=False)
    target = own_block * per_block + own_within
    row_pick = (target[None, :] == row_ids[:, None]).astype(jnp.bfloat16)
    order_ids = jnp.arange(orders, dtype=jnp.int32)
    order_pick = (order_table[:, None] == order_ids[None, :]).astype(jnp.bfloat16)
    by_order = jnp.einsum(
        "sm,cmi->csi", order_pick, fourier, preferred_element_type=jnp.float32
    ).astype(jnp.bfloat16)
    picked_rows = jnp.einsum(
        "csi,pi->csp", by_order, row_pick, preferred_element_type=jnp.float32
    ).astype(jnp.bfloat16)
    grouped = picked_rows.reshape(cols, owners, slots, blocks, per_block).transpose(3, 1, 4, 0, 2)
    grouped = grouped.reshape(blocks, owners, per_block, cols * slots)
    slot_ids = jnp.arange(per_block, dtype=jnp.int32)
    landing = (block_of == here_blk)[:, :, None] & (within[:, :, None] == slot_ids[None, None, :])
    arrival = jnp.sum(jnp.where(landing, table[:, :, None], 0), axis=1)
    received = lax.all_to_all(
        grouped.reshape(devices, per_block, cols * slots),
        ("blk", "order"),
        split_axis=0,
        concat_axis=0,
        tiled=True,
    )
    received = received.reshape(block_cycles, cols * slots)
    local_lat = arrival.reshape(block_cycles) - here_blk * block_cycles
    cycle_ids = jnp.arange(block_cycles, dtype=jnp.int32)
    placing = (local_lat[None, :] == cycle_ids[:, None]).astype(jnp.bfloat16)
    field = (
        jnp.dot(placing, received, preferred_element_type=jnp.float32)
        .astype(jnp.bfloat16)
        .reshape(block_cycles, cols, slots)
    )
    mixing = level_op[:, 0]
    chosen = skeleton[:, 0]
    coeff = climb(field, leaf_op, mixing, chosen, level_count)
    return jnp.einsum("jlk,jck->cjl", top_op, coeff, preferred_element_type=jnp.float32)


def solution(mesh):
    return jax.shard_map(
        per_device,
        mesh=mesh,
        in_specs=(
            P(None, None, ("blk", "order")),
            P(),
            P(),
            P("order", None, "blk"),
            P(None, "blk", "order", None, None),
            P(None, "blk", "order", None),
            P("order", "blk", None),
        ),
        out_specs=P(None, "order", "blk"),
        check_vma=False,
    )
```

profile of v0, /device:TPU:0, one launch (start us, length us, event | category | flops | bytes accessed | tf_op | source)
XLA Modules:
  0.0 110.3 jit_solution(13709033650705656841)
XLA Ops:
  0.0 0.0 copy-start
  0.0 1.0 reshape.121
  1.1 0.1 broadcast_compare_fusion
  1.2 10.5 %convert_reduce_fusion = s32[128,256]{1,0:T(8,128)S(1)} fusion(s32[128,256]{1,0:T(8,128)S(1)} %get-tuple-element.6, pred[256,256]{1,0:T(8,128)(4,1)S(1)} %iota_compare_fusion.32), kind=kLoop, calls=%fused_computation | loop fusion | flops 33521664 | bytes 327680 | tf_op jit(solution)/shard_map/reduce_sum | solution.py:51
  11.7 0.0 copy-done
  11.7 1.5 %convolution_convert_fusion = bf16[16,128,256]{2,1,0:T(8,128)(2,1)S(1)} fusion(bf16[16,128,256]{2,1,0:T(8,128)(2,1)S(1)} %copy-done, s32[256]{0:T(256)S(1)} %bitcast.46, s32[128]{0:T(128)} %param.9), kind=kOutput, calls=%fused_computation.16 | convolution fusion | flops 403783680 | bytes 2098688 | tf_op jit(solution)/shard_map/csi,pi->csp/dot_general | solution.py:64
  13.2 7.6 %reshape.122 = bf16[16,8,16,16,16]{4,3,2,1,0:T(8,128)(2,1)} reshape(bf16[16,128,256]{2,1,0:T(8,128)(2,1)S(1)} %convolution_convert_fusion) | data formatting | bytes 2097152 | tf_op jit(solution)/shard_map/reshape | solution.py:67
  20.7 13.8 %copy.13 = bf16[16,8,16,16,16]{2,0,4,1,3:T(8,128)(2,1)} copy(bf16[16,8,16,16,16]{4,3,2,1,0:T(8,128)(2,1)} %reshape.122) | data formatting | bytes 2097152 | tf_op jit(solution)/shard_map/reshape | solution.py:67
  34.5 11.0 %reshape_reshape.3 = bf16[128,16,256]{2,1,0:T(8,128)(2,1)} reshape(bf16[16,8,16,16,16]{4,3,2,1,0:T(8,128)(2,1)} %bitcast.43) | data formatting | bytes 2097152 | tf_op jit(solution)/shard_map/reshape;reshape | solution.py:73
  45.5 11.3 %all-to-all-start = ((bf16[128,16,256]{2,1,0:T(8,128)(2,1)}), bf16[128,16,256]{2,1,0:T(8,128)(2,1)S(1)}, u32[]{:S(2)}, u32[]{:S(2)}) async-start(bf16[128,16,256]{2,1,0:T(8,128)(2,1)} %reshape_reshape.3), calls=%async_computation | async-start | bytes 2097152 | tf_op jit(solution)/shard_map/all_to_all | solution.py:72
  56.9 2.2 %select_reduce_fusion = s32[128,16]{1,0:T(8,128)S(1)} fusion(s32[128,256]{1,0:T(8,128)S(1)} %reshape.121, s32[128,256]{1,0:T(8,128)S(1)} %convert_reduce_fusion, pred[128,256]{1,0:T(8,128)(4,1)S(1)} %get-tuple-element.5), kind=kLoop, calls=%fused_computation.9 | loop fusion | flops 2095104 | bytes 303104 | tf_op jit(solution)/shard_map/reduce_sum | solution.py:71
  59.1 0.1 sub.22
  59.2 16.5 %all-to-all-done = bf16[128,16,256]{2,1,0:T(8,128)(2,1)S(1)} async-done(((bf16[128,16,256]{2,1,0:T(8,128)(2,1)}), bf16[128,16,256]{2,1,0:T(8,128)(2,1)S(1)}, u32[]{:S(2)}, u32[]{:S(2)}) %all-to-all-start) | async-done | bytes 1048608 | tf_op jit(solution)/shard_map/all_to_all | solution.py:72
  75.7 3.5 %fusion.2 = bf16[2048,256]{0,1:T(8,128)(2,1)S(1)} fusion(bf16[2048,256]{1,0:T(8,128)(2,1)S(1)} %bitcast.45, s32[2048]{0:T(1024)S(1)} %sub.22), kind=kOutput, calls=%fused_computation.4 | convolution fusion | flops 2152202240 | bytes 2105344 | tf_op jit(solution)/shard_map/dot_general | solution.py:84
  79.2 0.0 copy-start.2
  79.2 0.0 copy-start.1
  79.2 5.8 %convolution_convert_fusion.2 = bf16[16,16,128]{2,1,0:T(8,128)(2,1)S(1)} fusion(bf16[16,128,2048]{2,1,0:T(8,128)(2,1)} %param.10, bf16[2048,16,16]{0,2,1:T(8,128)(2,1)S(1)} %bitcast.44), kind=kOutput, calls=%fused_computation.28 | convolution fusion | flops 134250496 | bytes 9502720 | tf_op jit(solution)/shard_map/jkr,rcj->jck/dot_general | solution.py:18
  85.1 0.0 collective-permute-start
  85.1 0.0 copy-done.2
  85.1 1.2 %collective-permute-done = bf16[16,16,128]{2,1,0:T(8,128)(2,1)S(1)} collective-permute-done((bf16[16,16,128]{2,1,0:T(8,128)(2,1)S(1)}, bf16[16,16,128]{2,1,0:T(8,128)(2,1)S(1)}, u32[]{:S(2)}, u32[]{:S(2)}) %collective-permute-start) | collective-permute-done | bytes 65568 | tf_op jit(solution)/shard_map/ppermute | solution.py:14
  86.3 0.0 copy-done.1
  86.3 0.4 fusion.23
  86.7 0.5 fusion.13
  87.2 0.6 collective-permute-start.1
  87.8 3.7 %collective-permute-done.1 = bf16[16,16,128]{2,1,0:T(8,128)(2,1)S(1)} collective-permute-done((bf16[16,16,128]{2,1,0:T(8,128)(2,1)S(1)}, bf16[16,16,128]{2,1,0:T(8,128)(2,1)S(1)}, u32[]{:S(2)}, u32[]{:S(2)}) %collective-permute-start.1) | collective-permute-done | bytes 65568 | tf_op jit(solution)/shard_map/ppermute | solution.py:14
  91.5 0.4 fusion.21
  91.9 0.5 fusion.14
  92.4 1.6 %collective-permute-start.2 = (bf16[16,16,128]{2,1,0:T(8,128)(2,1)S(1)}, bf16[16,16,128]{2,1,0:T(8,128)(2,1)S(1)}, u32[]{:S(2)}, u32[]{:S(2)}) collective-permute-start(bf16[16,16,128]{2,1,0:T(8,128)(2,1)S(1)} %fusion.14), channel_id=1, source_target_pairs={{0,32},{32,0},{8,40},{40,8},{16,48},{48,16},{24,56},{56,24},{64,96... | collective-permute-start | bytes 196616 | tf_op jit(solution)/shard_map/ppermute | solution.py:14
  94.0 4.2 %collective-permute-done.2 = bf16[16,16,128]{2,1,0:T(8,128)(2,1)S(1)} collective-permute-done((bf16[16,16,128]{2,1,0:T(8,128)(2,1)S(1)}, bf16[16,16,128]{2,1,0:T(8,128)(2,1)S(1)}, u32[]{:S(2)}, u32[]{:S(2)}) %collective-permute-start.2) | collective-permute-done | bytes 65568 | tf_op jit(solution)/shard_map/ppermute | solution.py:14
  98.2 0.4 fusion.19
  98.6 0.5 fusion.15
  99.1 0.1 collective-permute-start.3
  99.2 5.7 %collective-permute-done.3 = bf16[16,16,128]{2,1,0:T(8,128)(2,1)S(1)} collective-permute-done((bf16[16,16,128]{2,1,0:T(8,128)(2,1)S(1)}, bf16[16,16,128]{2,1,0:T(8,128)(2,1)S(1)}, u32[]{:S(2)}, u32[]{:S(2)}) %collective-permute-start.3) | collective-permute-done | bytes 65568 | tf_op jit(solution)/shard_map/ppermute | solution.py:14
  105.0 0.4 fusion.17
  105.3 3.4 %convolution_bitcast_fusion = f32[16,16,1024]{2,0,1:T(8,128)S(1)} fusion(bf16[16,1024,128]{2,1,0:T(8,128)(2,1)} %param.13, f32[16,16,128]{2,1,0:T(8,128)S(1)} %fusion.17, s32[16,128]{1,0:T(8,128)S(1)} %get-tuple-element.7, bf16[16,16,128]{2,1,0:T(8,128)(2,1)S(1)} %collective-permute-done.3, bf16[16,16,128]{2,1,0:T(8,128)(2,1)S(1)} %fusion.15), kind=kOutput, calls=%fused_computation.19 | convolution fusion | flops 84738048 | bytes 5513216 | tf_op jit(solution)/shard_map/jlk,jck->cjl/dot_general | solution.py:91
  108.7 1.6 %copy.15 = f32[16,16,1024]{2,1,0:T(8,128)} copy(f32[16,16,1024]{2,0,1:T(8,128)S(1)} %convolution_bitcast_fusion) | data formatting | bytes 2097152 | tf_op jit(solution)/shard_map/jlk,jck->cjl/transpose | solution.py:91
  (4 shorter events, 0.1 us)
Async XLA Ops:
  0.0 11.7 %copy-start = (bf16[16,128,256]{2,1,0:T(8,128)(2,1)S(1)}, bf16[16,128,256]{2,1,0:T(8,128)(2,1)}, u32[]{:S(2)}) copy-start(bf16[16,128,256]{2,1,0:T(8,128)(2,1)} %param.7) | copy-start | bytes 3145732
  45.5 30.1 %all-to-all-start = ((bf16[128,16,256]{2,1,0:T(8,128)(2,1)}), bf16[128,16,256]{2,1,0:T(8,128)(2,1)S(1)}, u32[]{:S(2)}, u32[]{:S(2)}) async-start(bf16[128,16,256]{2,1,0:T(8,128)(2,1)} %reshape_reshape.3), calls=%async_computation | async-start | bytes 2097152 | tf_op jit(solution)/shard_map/all_to_all | solution.py:72
  79.2 5.8 %copy-start.2 = (s32[4,1,16,128]{3,2,1,0:T(8,128)S(1)}, s32[4,1,16,128]{3,2,1,0:T(8,128)}, u32[]{:S(2)}) copy-start(s32[4,1,16,128]{3,2,1,0:T(8,128)} %param.12) | copy-start | bytes 98308
  79.2 7.1 %copy-start.1 = (bf16[4,1,16,128,256]{4,3,2,1,0:T(8,128)(2,1)S(1)}, bf16[4,1,16,128,256]{4,3,2,1,0:T(8,128)(2,1)}, u32[]{:S(2)}) copy-start(bf16[4,1,16,128,256]{4,3,2,1,0:T(8,128)(2,1)} %param.11) | copy-start | bytes 12582916
  85.1 1.3 %collective-permute-start = (bf16[16,16,128]{2,1,0:T(8,128)(2,1)S(1)}, bf16[16,16,128]{2,1,0:T(8,128)(2,1)S(1)}, u32[]{:S(2)}, u32[]{:S(2)}) collective-permute-start(bf16[16,16,128]{2,1,0:T(8,128)(2,1)S(1)} %convolution_convert_fusion.2), channel_id=1, source_target_pairs={{0,8},{8,0},{16,24},{24,16},{32,40},{40,32},{48,56},{56,48},{64,72... | collective-permute-start | bytes 196616 | tf_op jit(solution)/shard_map/ppermute | solution.py:14
  87.2 4.3 %collective-permute-start.1 = (bf16[16,16,128]{2,1,0:T(8,128)(2,1)S(1)}, bf16[16,16,128]{2,1,0:T(8,128)(2,1)S(1)}, u32[]{:S(2)}, u32[]{:S(2)}) collective-permute-start(bf16[16,16,128]{2,1,0:T(8,128)(2,1)S(1)} %fusion.13), channel_id=1, source_target_pairs={{0,16},{16,0},{8,24},{24,8},{32,48},{48,32},{40,56},{56,40},{64,80... | collective-permute-start | bytes 196616 | tf_op jit(solution)/shard_map/ppermute | solution.py:14
  92.4 5.8 %collective-permute-start.2 = (bf16[16,16,128]{2,1,0:T(8,128)(2,1)S(1)}, bf16[16,16,128]{2,1,0:T(8,128)(2,1)S(1)}, u32[]{:S(2)}, u32[]{:S(2)}) collective-permute-start(bf16[16,16,128]{2,1,0:T(8,128)(2,1)S(1)} %fusion.14), channel_id=1, source_target_pairs={{0,32},{32,0},{8,40},{40,8},{16,48},{48,16},{24,56},{56,24},{64,96... | collective-permute-start | bytes 196616 | tf_op jit(solution)/shard_map/ppermute | solution.py:14
  99.1 5.8 %collective-permute-start.3 = (bf16[16,16,128]{2,1,0:T(8,128)(2,1)S(1)}, bf16[16,16,128]{2,1,0:T(8,128)(2,1)S(1)}, u32[]{:S(2)}, u32[]{:S(2)}) collective-permute-start(bf16[16,16,128]{2,1,0:T(8,128)(2,1)S(1)} %fusion.15), channel_id=1, source_target_pairs={{0,64},{64,0},{8,72},{72,8},{16,80},{80,16},{24,88},{88,24},{32,96... | collective-permute-start | bytes 196616 | tf_op jit(solution)/shard_map/ppermute | solution.py:14
where the time goes:
time: 111 us; the launch traced here: 110 us
  local copies, waits for them, and re-layouts  35.1 us (32%)
  waiting for transfers between devices  31.3 us (28%)
  matrix products  17.2 us (15%)
  starting transfers between devices  13.6 us (12%)
  other arithmetic  12.9 us (12%)
    reshape x2, local copies, waits for them, and re-layouts, per_device(): picked_rows.reshape(cols, owners, slots, blocks, per_block)  21.3 us
    all_to_all x1, waiting for transfers between devices, per_device(): lax.all_to_all(grouped.reshape(devices, per_block, cols * slots), ('blk',...  16.5 us
    ppermute x4, waiting for transfers between devices, swapped(): return lax.ppermute(block, axis, route)  14.9 us
    all_to_all x1, starting transfers between devices, per_device(): lax.all_to_all(grouped.reshape(devices, per_block, cols * slots), ('blk',...  11.3 us
    another operation x1, local copies, waits for them, and re-layouts, per_device(): grouped.reshape(devices, per_block, cols * slots)  11 us
    reduce_sum x1, other arithmetic, per_device(): jnp.sum(((block_of[:, :, None] == block_of[:, None, :]) & earlier[None])....  10.5 us
    dot_general x1, matrix products, climb(): jnp.einsum('jkr,rcj->jck', leaf_part, field_part, preferred_element_type=...  5.81 us
    dot_general x1, matrix products, per_device(): jnp.dot(placing, received, preferred_element_type=jnp.float32)  3.54 us
  transfers between devices with their start and end apart: 5, of which 5 were waited for; matrix products, arithmetic and copies ran while one was open for 2% of the time, Pallas kernels for 0%

commit v1 on v0

v1 whole, which is shorter than its diff:
```python
import functools

import jax
import jax.numpy as jnp
from jax import lax
from jax.experimental import pallas as pl
from jax.experimental.pallas import tpu as pltpu
from jax.sharding import PartitionSpec as P

MESH = pl.DeviceIdType.MESH
BLKS, OWNERS, DEVICES = 16, 8, 128
COLS, ORDERS, ROWS, RPB = 16, 128, 256, 16
SLOTS, HALF, GROUPS = 16, 8, 2
RB, LB, KR, LEVELS = 2048, 1024, 128, 4
RB_SHIFT = 11
WIDE = COLS * HALF
CHUNKS = 8
BF, F32, I32 = jnp.bfloat16, jnp.float32, jnp.int32


def hops(k):
    kb, ko = k // OWNERS, k % OWNERS
    z = (kb >> 3) * 2 + (ko >> 2)
    ring = (0, 1, 2, 1)
    return ring[(kb >> 1) & 3] + ring[z] + ring[ko & 3]


PARTNERS = sorted(range(DEVICES), key=lambda k: (-hops(k), (k * 37) % DEVICES))
PARTNERS.remove(0)
PARTNERS.append(0)


def iota(shape, dim):
    return lax.broadcasted_iota(I32, shape, dim)


def ones_where(mask):
    return jnp.where(mask, 1.0, 0.0).astype(F32)


def dot(a, b):
    return jnp.dot(a, b, preferred_element_type=F32)


def dot_nt(a, b):
    return lax.dot_general(a, b, (((1,), (1,)), ((), ())), preferred_element_type=F32)


def kernel(
    fourier, lat, otab, leaf, level, skel, top, korder, out,
    fv, latv, otabv, leafv, mixv, skelv, topv, kordv, outv,
    wide, sendb, recvb, placing, total, field, products, comb,
    in_sem, send_sem, recv_sem, own_sem, x_send, x_recv, out_sem,
):
    b, o = lax.axis_index("blk"), lax.axis_index("order")
    me = b * OWNERS + o

    loads = [
        pltpu.make_async_copy(lat, latv, in_sem.at[0]),
        pltpu.make_async_copy(otab, otabv, in_sem.at[1]),
        pltpu.make_async_copy(fourier, fv, in_sem.at[2]),
        pltpu.make_async_copy(korder, kordv, in_sem.at[3]),
        pltpu.make_async_copy(skel, skelv, in_sem.at[4]),
        pltpu.make_async_copy(leaf, leafv, in_sem.at[5]),
        pltpu.make_async_copy(level, mixv.at[:, :, :, pl.ds(0, 2 * KR)], in_sem.at[6]),
    ]
    for s in range(SLOTS):
        loads.append(pltpu.make_async_copy(top.at[s], topv.at[:, pl.ds(s * KR, KR)], in_sem.at[7 + s]))
    for copy in loads[:3]:
        copy.start()

    barrier = pltpu.get_barrier_semaphore()

    def greet(i, carry):
        pl.semaphore_signal(
            barrier, inc=1, device_id=(b ^ (i // OWNERS), o ^ (i % OWNERS)), device_id_type=MESH
        )
        return carry

    lax.fori_loop(1, DEVICES, greet, 0)
    for copy in loads[3:]:
        copy.start()

    loads[0].wait()
    own = jnp.concatenate([latv[pl.ds(2 * me, 1), :], latv[pl.ds(2 * me + 1, 1), :]], axis=1)
    own_block = own >> RB_SHIFT
    in_block = ones_where(iota((BLKS, ROWS), 0) == own_block)
    earlier = ones_where(iota((ROWS, ROWS), 0) < iota((ROWS, ROWS), 1)).astype(BF)
    rank = jnp.sum(in_block * dot(in_block.astype(BF), earlier), axis=0, keepdims=True)
    target = own_block * RPB + rank.astype(I32)
    row_pick = ones_where(iota((ROWS, ROWS), 0) == target).astype(BF)

    loads[1].wait()
    order_pick = jnp.transpose(ones_where(iota((ORDERS, ORDERS), 0) == otabv[...])).astype(BF)
    loads[2].wait()
    for c in range(COLS):
        by_slot = dot(order_pick, fv[c])
        wide[:, c * HALF:(c + 1) * HALF, :] = by_slot.reshape(OWNERS * GROUPS, HALF, ROWS)

    def sort_rows(i, carry):
        both = wide[pl.ds(GROUPS * i, GROUPS)].reshape(GROUPS * WIDE, ROWS).astype(BF)
        rows = dot_nt(row_pick, both).astype(BF)
        for g in range(GROUPS):
            sendb[g, i] = rows[:, g * WIDE:(g + 1) * WIDE]
        return carry

    lax.fori_loop(0, OWNERS, sort_rows, 0)

    pl.semaphore_wait(barrier, DEVICES - 1)
    for g in range(GROUPS):
        for t, k in enumerate(PARTNERS):
            kb, ko = b ^ (k // OWNERS), o ^ (k % OWNERS)
            src = sendb.at[g, ko, pl.ds(kb * RPB, RPB), :]
            dst = recvb.at[g, pl.ds(t * RPB, RPB), :]
            if k == 0:
                pltpu.make_async_copy(src, dst, own_sem.at[g]).start()
            else:
                pltpu.make_async_remote_copy(
                    src, dst, send_sem, recv_sem.at[g, t // (DEVICES // CHUNKS)],
                    device_id=(kb, ko), device_id_type=MESH,
                ).start()

    lat_t = jnp.concatenate(
        [jnp.transpose(latv[pl.ds(h, DEVICES, stride=2), :].astype(F32)) for h in range(2)], axis=0
    ).astype(I32)
    here = (lat_t >> RB_SHIFT) == b
    local = lat_t & (RB - 1)
    later = ones_where(iota((ROWS, ROWS), 1) < iota((ROWS, ROWS), 0)).astype(BF)
    ranks = dot(later, ones_where(here).astype(BF)).astype(I32)
    ranks = jnp.where(here, ranks, -1)
    by_rank = jnp.concatenate(
        [jnp.sum(jnp.where(ranks == p, local, 0), axis=0, keepdims=True) for p in range(RPB)], axis=0
    )
    parts = jnp.concatenate([by_rank >> 4, by_rank & 15], axis=0).astype(F32).astype(BF)
    loads[3].wait()
    sender = ones_where(iota((DEVICES, RB), 0) == (kordv[...] ^ me)).astype(BF)
    spread = dot(parts, sender)
    keep = iota((RPB, RB), 0) == (iota((RPB, RB), 1) & (RPB - 1))
    high = jnp.sum(jnp.where(keep, spread[:RPB], 0.0), axis=0, keepdims=True)
    low = jnp.sum(jnp.where(keep, spread[RPB:], 0.0), axis=0, keepdims=True)
    place = (high * 16.0 + low).astype(I32)
    step = RB // CHUNKS
    for n in range(CHUNKS):
        at = place[:, n * step:(n + 1) * step]

        def fill(i, carry):
            mask = (iota((256, step), 0) + i * 256) == at
            placing[n, pl.ds(pl.multiple_of(i * 256, 256), 256), :] = ones_where(mask).astype(BF)
            return carry

        lax.fori_loop(0, RB // 256, fill, 0)

    loads[4].wait()
    pad = jnp.zeros((KR - LEVELS * SLOTS, KR), F32)
    lists = jnp.transpose(jnp.concatenate([skelv[...].astype(F32), pad], axis=0)).astype(I32)
    for j in range(LEVELS):
        for s in range(SLOTS):
            column = lists[:, j * SLOTS + s:j * SLOTS + s + 1]
            mixv[j, s, :, 2 * KR:] = ones_where(iota((KR, 2 * KR), 1) == column).astype(BF)

    lane_slot = iota((KR, WIDE), 1) & (HALF - 1)

    def own_lanes(rows):
        kept = rows[:KR]
        for s in range(1, HALF):
            kept = jnp.where(lane_slot == s, rows[s * KR:(s + 1) * KR], kept)
        return kept

    def exchange(j, g, coeff):
        comb[j, g, :KR, :] = coeff.astype(BF)
        copy = pltpu.make_async_remote_copy(
            comb.at[j, g, pl.ds(0, KR), :], comb.at[j, g, pl.ds(KR, KR), :],
            x_send.at[j, g], x_recv.at[j, g], device_id=(b ^ (1 << j), o), device_id_type=MESH,
        )
        copy.start()
        return copy

    def leaf_step(g):
        total[...] = jnp.zeros_like(total)
        for n in range(CHUNKS):
            rows = step if n < CHUNKS - 1 else step - RPB
            landed = recvb.at[g, pl.ds(n * step, rows), :]
            pltpu.make_async_copy(landed, landed, recv_sem.at[g, n]).wait()
            if n == CHUNKS - 1:
                mine = recvb.at[g, pl.ds(RB - RPB, RPB), :]
                pltpu.make_async_copy(mine, mine, own_sem.at[g]).wait()
            total[...] += dot(placing[n], recvb[g, n * step:(n + 1) * step, :])
        field[...] = total[...].astype(BF)
        products[...] = dot(leafv[g * HALF:(g + 1) * HALF].reshape(HALF * KR, RB), field[...])
        return own_lanes(products[...])

    def level_step(j, g):
        pair = comb[j, g]
        both = jnp.concatenate([pair, pair], axis=0)
        products[...] = dot(mixv[j, g * HALF:(g + 1) * HALF].reshape(HALF * KR, 4 * KR), both)
        return own_lanes(products[...])

    def top_step(g, coeff):
        turned = jnp.transpose(coeff)
        row_slot = iota((WIDE, KR), 0) & (HALF - 1)
        spread_rows = jnp.concatenate(
            [jnp.where(row_slot == s, turned, 0.0).astype(BF) for s in range(HALF)], axis=1
        )
        res = dot_nt(spread_rows, topv[:, g * HALF * KR:(g + 1) * HALF * KR])
        outv[:, g * HALF:(g + 1) * HALF, :] = res.reshape(COLS, HALF, LB)
        copy = pltpu.make_async_copy(
            outv.at[:, pl.ds(g * HALF, HALF), :], out.at[:, pl.ds(g * HALF, HALF), :], out_sem.at[g]
        )
        copy.start()
        return copy

    for copy in loads[5:]:
        copy.wait()
    copies = [[None] * GROUPS for _ in range(LEVELS)]
    for g in range(GROUPS):
        copies[0][g] = exchange(0, g, leaf_step(g))
    coeffs = [None] * GROUPS
    for j in range(LEVELS):
        for g in range(GROUPS):
            copies[j][g].wait()
            coeff = level_step(j, g)
            if j + 1 < LEVELS:
                copies[j + 1][g] = exchange(j + 1, g, coeff)
            else:
                coeffs[g] = coeff.astype(BF).astype(F32)
    stores = [top_step(g, coeffs[g]) for g in range(GROUPS)]
    sent = sendb.at[0, pl.ds(0, OWNERS), :, :]
    for g in range(GROUPS):
        left = recvb.at[g, pl.ds(0, RB - RPB), :]
        pltpu.make_async_copy(left, left, send_sem).wait()
    for copy in stores:
        copy.wait()


def per_device(fourier, cycle_lat, order_table, leaf_op, level_op, skeleton, top_op):
    positions = jnp.repeat(jnp.array(PARTNERS, I32), RPB).reshape(1, RB)
    any_space = pl.BlockSpec(memory_space=pl.ANY)
    dma = pltpu.SemaphoreType.DMA
    return pl.pallas_call(
        kernel,
        out_shape=jax.ShapeDtypeStruct((COLS, SLOTS, LB), F32),
        in_specs=[any_space] * 8,
        out_specs=any_space,
        scratch_shapes=[
            pltpu.VMEM((COLS, ORDERS, ROWS), BF),
            pltpu.VMEM((2 * DEVICES, 128), I32),
            pltpu.VMEM((1, ORDERS), I32),
            pltpu.VMEM((SLOTS, KR, RB), BF),
            pltpu.VMEM((LEVELS, SLOTS, KR, 4 * KR), BF),
            pltpu.VMEM((LEVELS * SLOTS, KR), I32),
            pltpu.VMEM((LB, SLOTS * KR), BF),
            pltpu.VMEM((1, RB), I32),
            pltpu.VMEM((COLS, SLOTS, LB), F32),
            pltpu.VMEM((OWNERS * GROUPS, WIDE, ROWS), F32),
            pltpu.VMEM((GROUPS, OWNERS, ROWS, WIDE), BF),
            pltpu.VMEM((GROUPS, RB, WIDE), BF),
            pltpu.VMEM((CHUNKS, RB, RB // CHUNKS), BF),
            pltpu.VMEM((RB, WIDE), F32),
            pltpu.VMEM((RB, WIDE), BF),
            pltpu.VMEM((HALF * KR, WIDE), F32),
            pltpu.VMEM((LEVELS, GROUPS, 2 * KR, WIDE), BF),
            dma((7 + SLOTS,)),
            dma,
            dma((GROUPS, CHUNKS)),
            dma((GROUPS,)),
            dma((LEVELS, GROUPS)),
            dma((LEVELS, GROUPS)),
            dma((GROUPS,)),
        ],
        compiler_params=pltpu.CompilerParams(
            collective_id=0, has_side_effects=True, vmem_limit_bytes=58 * 1024 * 1024
        ),
    )(
        fourier,
        cycle_lat.reshape(2 * DEVICES, 128),
        order_table.reshape(1, ORDERS),
        leaf_op,
        level_op[:, 0],
        skeleton.reshape(LEVELS * SLOTS, KR),
        top_op,
        positions,
    )


def solution(mesh):
    return jax.shard_map(
        per_device,
        mesh=mesh,
        in_specs=(
            P(None, None, ("blk", "order")),
            P(),
            P(),
            P("order", None, "blk"),
            P(None, "blk", "order", None, None),
            P(None, "blk", "order", None),
            P("order", "blk", None),
        ),
        out_specs=P(None, "order", "blk"),
        check_vma=False,
    )
```

time: 111 us -> 53 us (0.48)
  Pallas kernels: 0 us -> 49.1 us
  local copies, waits for them, and re-layouts: 35.1 us -> 3.74 us
  waiting for transfers between devices: 31.3 us -> 0 us
  matrix products: 17.2 us -> 0 us
  starting transfers between devices: 13.6 us -> 0 us
  other arithmetic: 12.9 us -> 0 us
    pallas_call x0 -> x1, Pallas kernels: none -> 49.1 us  [per_device(): pl.pallas_call(kernel, out_shape=jax.ShapeDtypeStruct((COLS, SLOTS, LB),...]
    reshape x3 -> x0, local copies, waits for them, and re-layouts: 22.4 us -> none  [the longest x2 21.3 us: per_device(): picked_rows.reshape(cols, owners, slots, blocks, per_block)]
    dot_general x11 -> x0, matrix products: 17.2 us -> none  [the longest x1 5.81 us: climb(): jnp.einsum('jkr,rcj->jck', leaf_part, field_part, preferred_element_type=...]
    all_to_all x1 -> x0, waiting for transfers between devices: 16.5 us -> none  [per_device(): lax.all_to_all(grouped.reshape(devices, per_block, cols * slots), ('blk',...]
    ppermute x4 -> x0, waiting for transfers between devices: 14.9 us -> none  [swapped(): return lax.ppermute(block, axis, route)]
    reduce_sum x2 -> x0, other arithmetic: 12.7 us -> none  [the longest x1 10.5 us: per_device(): jnp.sum(((block_of[:, :, None] == block_of[:, None, :]) & earlier[None])....]
    all_to_all x1 -> x0, starting transfers between devices: 11.3 us -> none  [per_device(): lax.all_to_all(grouped.reshape(devices, per_block, cols * slots), ('blk',...]
    another operation x1, local copies, waits for them, and re-layouts: 11 us -> 0.7 us  [per_device(): positions = jnp.repeat(jnp.array(PARTNERS, I32), RPB).reshape(1, RB)]
  transfers between devices with their start and end apart: 5 -> 0, of which waited for: 5 -> 0; matrix products, arithmetic and copies ran while one was open for 2% -> 0% of each run, Pallas kernels for 0% -> 0%
where the time goes in v1:
time: 53 us; the launch traced here: 52.9 us
  Pallas kernels  49.1 us (93%)
  local copies, waits for them, and re-layouts  3.74 us (7%)
    pallas_call x1, Pallas kernels, per_device(): pl.pallas_call(kernel, out_shape=jax.ShapeDtypeStruct((COLS, SLOTS, LB),...  49.1 us
    unnamed x1, local copies, waits for them, and re-layouts  2.31 us

profile of v1, /device:TPU:0, one launch (start us, length us, event | category | flops | bytes accessed | tf_op | source)
XLA Modules:
  0.0 52.9 jit_solution(14926061897831367156)
XLA Ops:
  0.0 0.7 %broadcast_in_dim.3 = s32[128,16]{1,0:T(8,128)S(1)} broadcast(s32[128]{0:T(128)} %constant.2.clone), dimensions={0} | broadcast | bytes 8704 | tf_op jit(solution)/shard_map/broadcast_in_dim | solution.py:236
  0.7 0.7 %reshape_reshape.3.korder = s32[1,2048]{1,0:T(1,128)} reshape(s32[128,16]{1,0:T(8,128)S(1)} %broadcast_in_dim.3) | data formatting | bytes 16384 | tf_op jit(solution)/shard_map/reshape;reshape | solution.py:236
  1.4 49.1 %shard_map.82 = f32[16,16,1024]{2,1,0:T(8,128)} custom-call(bf16[16,128,256]{2,1,0:T(8,128)(2,1)} %fourier.1, s32[256,128]{1,0:T(8,128)} %bitcast.5, s32[1,128]{1,0:T(1,128)} %bitcast.7, bf16[16,128,2048]{2,1,0:T(8,128)(2,1)} %leaf.1, bf16[4,16,128,256]{3,2,1,0:T(8,128)(2,1)} %bitcast.4, s32[64,128]{1,0:T(8,128)} %bitcast.6, bf16[16,1024,128]{2,1,0:T(8,128)(2,1)} %top.1, ...), custom_call_target="tpu_custom_call" | custom-call | tf_op jit(solution)/shard_map/pallas_call | solution.py:239
  50.5 2.3 %copy.10 = f32[16,16,1024]{2,1,0:T(8,128)} copy(f32[16,16,1024]{2,1,0:T(8,128)} %shard_map.82) | data formatting | bytes 2097152

commit v2 on v1

v2 whole, which is shorter than its diff:
```python
import functools

import jax
import jax.numpy as jnp
import numpy as np
from jax import lax
from jax.experimental import pallas as pl
from jax.experimental.pallas import tpu as pltpu
from jax.sharding import PartitionSpec as P

MESH = pl.DeviceIdType.MESH
BLKS, OWNERS, DEVICES = 16, 8, 128
COLS, ORDERS, ROWS, RPB = 16, 128, 256, 16
SLOTS, HALF, GROUPS = 16, 8, 2
RB, LB, KR, LEVELS = 2048, 1024, 128, 4
RB_SHIFT = 11
WIDE = COLS * HALF
CHUNKS, TAIL, TILE, PART = 8, 2, 256, 256
HEAD = CHUNKS - TAIL
BF, F32, I32 = jnp.bfloat16, jnp.float32, jnp.int32


def hops(k):
    kb, ko = k // OWNERS, k % OWNERS
    z = (kb >> 3) * 2 + (ko >> 2)
    ring = (0, 1, 2, 1)
    return ring[(kb >> 1) & 3] + ring[z] + ring[ko & 3]


PARTNERS = sorted(range(DEVICES), key=lambda k: (-hops(k), (k * 37) % DEVICES))
PARTNERS.remove(0)
PARTNERS.append(0)


ONE, ZERO = np.array(1, BF), np.array(0, BF)


def iota(shape, dim):
    return lax.broadcasted_iota(I32, shape, dim)


def ones_where(mask):
    return jnp.where(mask, 1.0, 0.0).astype(F32)


def dot(a, b):
    return jnp.dot(a, b, preferred_element_type=F32)


def dot_nt(a, b):
    return lax.dot_general(a, b, (((1,), (1,)), ((), ())), preferred_element_type=F32)


def analyse(
    fourier, lat, otab, leaf, level, skel, korder, out,
    fv, latv, otabv, leafv, mixv, skelv, kordv,
    wide, sendb, recvb, placing, turned, total, field, products, comb,
    in_sem, send_sem, recv_sem, own_sem, x_send, x_recv,
):
    b, o = lax.axis_index("blk"), lax.axis_index("order")
    me = b * OWNERS + o

    loads = [
        pltpu.make_async_copy(lat, latv, in_sem.at[0]),
        pltpu.make_async_copy(otab, otabv, in_sem.at[1]),
        pltpu.make_async_copy(fourier, fv, in_sem.at[2]),
        pltpu.make_async_copy(korder, kordv, in_sem.at[3]),
        pltpu.make_async_copy(skel, skelv, in_sem.at[4]),
        pltpu.make_async_copy(leaf, leafv, in_sem.at[5]),
        pltpu.make_async_copy(
            level.at[:, :, :, pl.ds(0, KR)], mixv.at[:, :, :, pl.ds(0, KR)], in_sem.at[6]
        ),
        pltpu.make_async_copy(
            level.at[:, :, :, pl.ds(KR, KR)], mixv.at[:, :, :, pl.ds(2 * KR, KR)], in_sem.at[7]
        ),
    ]
    for copy in loads[:3]:
        copy.start()

    barrier = pltpu.get_barrier_semaphore()
    for k in PARTNERS[:-1]:
        pl.semaphore_signal(
            barrier, inc=1, device_id=(b ^ (k // OWNERS), o ^ (k % OWNERS)), device_id_type=MESH
        )
    for copy in loads[3:]:
        copy.start()

    loads[0].wait()
    own = jnp.concatenate([latv[pl.ds(2 * me, 1), :], latv[pl.ds(2 * me + 1, 1), :]], axis=1)
    own_block = own >> RB_SHIFT
    in_block = ones_where(iota((BLKS, ROWS), 0) == own_block)
    earlier = ones_where(iota((ROWS, ROWS), 0) < iota((ROWS, ROWS), 1)).astype(BF)
    rank = jnp.sum(in_block * dot(in_block.astype(BF), earlier), axis=0, keepdims=True)
    target = own_block * RPB + rank.astype(I32)
    row_pick = ones_where(iota((ROWS, ROWS), 0) == target).astype(BF)

    loads[1].wait()
    order_pick = jnp.transpose(ones_where(iota((ORDERS, ORDERS), 0) == otabv[...])).astype(BF)
    loads[2].wait()
    for c in range(COLS):
        by_slot = dot(order_pick, fv[c])
        wide[:, c * HALF:(c + 1) * HALF, :] = by_slot.reshape(OWNERS * GROUPS, HALF, ROWS)

    def sort_rows(i, carry):
        both = wide[pl.ds(GROUPS * i, GROUPS)].reshape(GROUPS * WIDE, ROWS).astype(BF)
        sendb[i] = dot_nt(row_pick, both).astype(BF)
        return carry

    lax.fori_loop(0, OWNERS, sort_rows, 0)

    def skeleton_step():
        loads[4].wait()
        pad = jnp.zeros((KR - LEVELS * SLOTS, KR), F32)
        lists = jnp.transpose(jnp.concatenate([skelv[...].astype(F32), pad], axis=0)).astype(BF)
        lanes = iota((KR, 2 * KR), 1).astype(F32).astype(BF)
        for j in range(LEVELS):
            for s in range(SLOTS):
                column = lists[:, j * SLOTS + s:j * SLOTS + s + 1]
                chosen = jnp.where(lanes == column, ONE, ZERO)
                mixv[j, s, :, KR:2 * KR] = chosen[:, :KR]
                mixv[j, s, :, 3 * KR:] = chosen[:, KR:]

    def place_step():
        lat_t = jnp.concatenate(
            [jnp.transpose(latv[pl.ds(h, DEVICES, stride=2), :].astype(F32)) for h in range(2)], axis=0
        ).astype(I32)
        here = (lat_t >> RB_SHIFT) == b
        local = lat_t & (RB - 1)
        later = ones_where(iota((ROWS, ROWS), 1) < iota((ROWS, ROWS), 0)).astype(BF)
        ranks = dot(later, ones_where(here).astype(BF)).astype(I32)
        ranks = jnp.where(here, ranks, -1)
        by_rank = jnp.concatenate(
            [jnp.sum(jnp.where(ranks == p, local, 0), axis=0, keepdims=True) for p in range(RPB)], axis=0
        )
        parts = jnp.concatenate([by_rank >> 4, by_rank & 15], axis=0).astype(F32).astype(BF)
        loads[3].wait()
        sender = ones_where(iota((DEVICES, RB), 0) == (kordv[...] ^ me)).astype(BF)
        spread = dot(parts, sender)
        keep = iota((RPB, RB), 0) == (iota((RPB, RB), 1) & (RPB - 1))
        high = jnp.sum(jnp.where(keep, spread[:RPB], 0.0), axis=0, keepdims=True)
        low = jnp.sum(jnp.where(keep, spread[RPB:], 0.0), axis=0, keepdims=True)
        place = high * 16.0 + low
        near = iota((TILE, TILE), 0).astype(F32).astype(BF)
        for n in range(CHUNKS):
            for i in range(RB // TILE):
                at = (place[:, n * TILE:(n + 1) * TILE] - float(i * TILE)).astype(BF)
                placing[n, i * TILE:(i + 1) * TILE, :] = jnp.where(near == at, ONE, ZERO)

    pl.semaphore_wait(barrier, DEVICES - 1)
    for t, k in enumerate(PARTNERS):
        kb, ko = b ^ (k // OWNERS), o ^ (k % OWNERS)
        src = sendb.at[ko, pl.ds(kb * RPB, RPB), :]
        dst = recvb.at[pl.ds(t * RPB, RPB), :]
        if k == 0:
            pltpu.make_async_copy(src, dst, own_sem).start()
        else:
            pltpu.make_async_remote_copy(
                src, dst, send_sem, recv_sem.at[t // (DEVICES // CHUNKS)],
                device_id=(kb, ko), device_id_type=MESH,
            ).start()

    skeleton_step()
    place_step()

    lane_slot = iota((KR, WIDE), 1) & (HALF - 1)

    def own_lanes(rows):
        kept = rows[:KR]
        for s in range(1, HALF):
            kept = jnp.where(lane_slot == s, rows[s * KR:(s + 1) * KR], kept)
        return kept

    def exchange(j, g, coeff):
        comb[j, g, :KR, :] = coeff.astype(BF)
        copy = pltpu.make_async_remote_copy(
            comb.at[j, g, pl.ds(0, KR), :], comb.at[j, g, pl.ds(KR, KR), :],
            x_send.at[j, g], x_recv.at[j, g], device_id=(b ^ (1 << j), o), device_id_type=MESH,
        )
        copy.start()
        return copy

    def slot_rows(ref, g):
        return ref[g * HALF:(g + 1) * HALF].reshape(HALF * KR, ref.shape[2])

    def lanes_of(g):
        return slice(g * WIDE, (g + 1) * WIDE)

    loads[5].wait()
    for i in range(SLOTS // 4):
        some = leafv[4 * i:4 * i + 4].reshape(4 * KR, RB)
        for n in range(TAIL):
            turned[4 * i * KR:4 * (i + 1) * KR, n * TILE:(n + 1) * TILE] = dot(
                some, placing[HEAD + n]
            ).astype(BF)

    def landed(n):
        rows = TILE if n < CHUNKS - 1 else TILE - RPB
        part = recvb.at[pl.ds(n * TILE, rows), :]
        pltpu.make_async_copy(part, part, recv_sem.at[n]).wait()

    for n in range(HEAD):
        landed(n)
        moved = dot(placing[n], recvb[n * TILE:(n + 1) * TILE, :])
        if n == 0:
            total[...] = moved
        elif n < HEAD - 1:
            total[...] += moved
        else:
            field[...] = (total[...] + moved).astype(BF)
    partial = []
    for g in range(GROUPS):
        products[...] = dot(slot_rows(leafv, g), field[:, lanes_of(g)])
        partial.append(own_lanes(products[...]))

    def level_part(j, g, half):
        x = comb[j, g, half * KR:(half + 1) * KR, :]
        rows = slot_rows(mixv.at[j], g)[:, 2 * half * KR:2 * (half + 1) * KR]
        products[...] = dot(rows, jnp.concatenate([x, x], axis=0))
        return own_lanes(products[...])

    for n in range(HEAD, CHUNKS):
        landed(n)
    mine = recvb.at[pl.ds(RB - RPB, RPB), :]
    pltpu.make_async_copy(mine, mine, own_sem).wait()
    copies = [[None] * GROUPS for _ in range(LEVELS)]
    for g in range(GROUPS):
        rows = turned[g * HALF * KR:(g + 1) * HALF * KR, :]
        products[...] = dot(rows, recvb[HEAD * TILE:, lanes_of(g)])
        copies[0][g] = exchange(0, g, partial[g] + own_lanes(products[...]))
    loads[6].wait()
    loads[7].wait()
    for j in range(LEVELS):
        partial = [level_part(j, g, 0) for g in range(GROUPS)]
        for g in range(GROUPS):
            copies[j][g].wait_recv()
            coeff = partial[g] + level_part(j, g, 1)
            if j + 1 < LEVELS:
                copies[j + 1][g] = exchange(j + 1, g, coeff)
            else:
                out[g] = jnp.transpose(coeff).astype(BF)
    for row in copies:
        for copy in row:
            copy.wait_send()
    left = recvb.at[pl.ds(0, RB - RPB), :]
    pltpu.make_async_copy(left, left, send_sem).wait()


def expand(coeff, top, out, block, sem):
    row_slot = iota((WIDE, KR), 0) & (HALF - 1)
    spread = []
    for g in range(GROUPS):
        rows = coeff[g].astype(F32)
        spread.append(jnp.concatenate(
            [jnp.where(row_slot == s, rows, 0.0).astype(BF) for s in range(HALF)], axis=1
        ))
    stores = []
    for n in range(LB // PART):
        at = pl.ds(n * PART, PART)
        for g in range(GROUPS):
            wanted = jnp.concatenate([top[g * HALF + s, at, :] for s in range(HALF)], axis=1)
            block[:, g * HALF:(g + 1) * HALF, at] = dot_nt(spread[g], wanted).reshape(COLS, HALF, PART)
        copy = pltpu.make_async_copy(block.at[:, :, at], out.at[:, :, at], sem.at[n])
        copy.start()
        stores.append(copy)
    for copy in stores:
        copy.wait()


def per_device(fourier, cycle_lat, order_table, leaf_op, level_op, skeleton, top_op):
    positions = jnp.asarray(np.repeat(np.array(PARTNERS, np.int32), RPB).reshape(1, RB))
    hbm = pl.BlockSpec(memory_space=pltpu.HBM)
    dma = pltpu.SemaphoreType.DMA
    coeff = pl.pallas_call(
        analyse,
        out_shape=jax.ShapeDtypeStruct((GROUPS, WIDE, KR), BF),
        in_specs=[hbm] * 7,
        out_specs=pl.BlockSpec(memory_space=pltpu.VMEM),
        scratch_shapes=[
            pltpu.VMEM((COLS, ORDERS, ROWS), BF),
            pltpu.VMEM((2 * DEVICES, 128), I32),
            pltpu.VMEM((1, ORDERS), I32),
            pltpu.VMEM((SLOTS, KR, RB), BF),
            pltpu.VMEM((LEVELS, SLOTS, KR, 4 * KR), BF),
            pltpu.VMEM((LEVELS * SLOTS, KR), I32),
            pltpu.VMEM((1, RB), I32),
            pltpu.VMEM((OWNERS * GROUPS, WIDE, ROWS), F32),
            pltpu.VMEM((OWNERS, ROWS, GROUPS * WIDE), BF),
            pltpu.VMEM((RB, GROUPS * WIDE), BF),
            pltpu.VMEM((CHUNKS, RB, TILE), BF),
            pltpu.VMEM((SLOTS * KR, TAIL * TILE), BF),
            pltpu.VMEM((RB, GROUPS * WIDE), F32),
            pltpu.VMEM((RB, GROUPS * WIDE), BF),
            pltpu.VMEM((HALF * KR, WIDE), F32),
            pltpu.VMEM((LEVELS, GROUPS, 2 * KR, WIDE), BF),
            dma((8,)),
            dma,
            dma((CHUNKS,)),
            dma,
            dma((LEVELS, GROUPS)),
            dma((LEVELS, GROUPS)),
        ],
        compiler_params=pltpu.CompilerParams(
            collective_id=0, has_side_effects=True, vmem_limit_bytes=58 * 1024 * 1024
        ),
    )(
        fourier,
        cycle_lat.reshape(2 * DEVICES, 128),
        order_table.reshape(1, ORDERS),
        leaf_op,
        level_op[:, 0],
        skeleton.reshape(LEVELS * SLOTS, KR),
        positions,
    )
    return pl.pallas_call(
        expand,
        out_shape=jax.ShapeDtypeStruct((COLS, SLOTS, LB), F32),
        in_specs=[pl.BlockSpec(memory_space=pltpu.VMEM)] * 2,
        out_specs=pl.BlockSpec(memory_space=pl.ANY),
        scratch_shapes=[pltpu.VMEM((COLS, SLOTS, LB), F32), dma((LB // PART,))],
        compiler_params=pltpu.CompilerParams(vmem_limit_bytes=16 * 1024 * 1024),
    )(coeff, top_op)


def solution(mesh):
    return jax.shard_map(
        per_device,
        mesh=mesh,
        in_specs=(
            P(None, None, ("blk", "order")),
            P(),
            P(),
            P("order", None, "blk"),
            P(None, "blk", "order", None, None),
            P(None, "blk", "order", None),
            P("order", "blk", None),
        ),
        out_specs=P(None, "order", "blk"),
        check_vma=False,
    )
```

time: 53 us -> 46.5 us (0.88)
  Pallas kernels: 49.1 us -> 45.5 us
  local copies, waits for them, and re-layouts: 3.74 us -> 0.84 us
    pallas_call x1 -> x2, Pallas kernels: 49.1 us -> 45.5 us  [the longest x1 43.3 us: per_device(): pl.pallas_call(analyse, out_shape=jax.ShapeDtypeStruct((GROUPS, WIDE, KR)...]
    unnamed x1 -> x4, local copies, waits for them, and re-layouts: 2.31 us -> 0.84 us
    broadcast_in_dim x1 -> x0, local copies, waits for them, and re-layouts: 0.73 us -> none  [per_device(): positions = jnp.repeat(jnp.array(PARTNERS, I32), RPB).reshape(1, RB)]
    another operation x1 -> x0, local copies, waits for them, and re-layouts: 0.7 us -> none  [per_device(): positions = jnp.repeat(jnp.array(PARTNERS, I32), RPB).reshape(1, RB)]
where the time goes in v2:
time: 46.5 us; the launch traced here: 46.3 us
  Pallas kernels  45.5 us (98%)
  local copies, waits for them, and re-layouts  0.84 us (2%)
    pallas_call x1, Pallas kernels, per_device(): pl.pallas_call(analyse, out_shape=jax.ShapeDtypeStruct((GROUPS, WIDE, KR)...  43.3 us
    pallas_call x1, Pallas kernels, per_device(): pl.pallas_call(expand, out_shape=jax.ShapeDtypeStruct((COLS, SLOTS, LB),...  2.22 us

profile of v2, /device:TPU:0, one launch (start us, length us, event | category | flops | bytes accessed | tf_op | source)
XLA Modules:
  0.0 46.3 jit_solution(7381212579542963523)
XLA Ops:
  0.0 0.0 copy-start
  0.0 43.3 %shard_map.82.coeff = bf16[2,128,128]{2,1,0:T(8,128)(2,1)} custom-call(bf16[16,128,256]{2,1,0:T(8,128)(2,1)} %fourier.1, s32[256,128]{1,0:T(8,128)} %bitcast.5, s32[1,128]{1,0:T(1,128)} %bitcast.7, bf16[16,128,2048]{2,1,0:T(8,128)(2,1)} %leaf.1, bf16[4,16,128,256]{3,2,1,0:T(8,128)(2,1)} %bitcast.4, s32[64,128]{1,0:T(8,128)} %bitcast.6, ...), custom_call_target="tpu_custom_call" | custom-call | tf_op jit(solution)/shard_map/pallas_call | solution.py:273
  43.3 0.0 copy-done
  43.3 0.0 copy-start.1
  43.3 0.8 %copy-done.1 = bf16[2,128,128]{2,1,0:T(8,128)(2,1)S(1)} copy-done((bf16[2,128,128]{2,1,0:T(8,128)(2,1)S(1)}, bf16[2,128,128]{2,1,0:T(8,128)(2,1)}, u32[]{:S(2)}) %copy-start.1) | copy-done | bytes 65560
  44.1 2.2 %shard_map.83 = f32[16,16,1024]{2,1,0:T(8,128)} custom-call(bf16[2,128,128]{2,1,0:T(8,128)(2,1)S(1)} %copy-done.1, bf16[16,1024,128]{2,1,0:T(8,128)(2,1)S(1)} %copy-done), custom_call_target="tpu_custom_call" | custom-call | tf_op jit(solution)/shard_map/pallas_call | solution.py:314
Async XLA Ops:
  0.0 43.3 %copy-start = (bf16[16,1024,128]{2,1,0:T(8,128)(2,1)S(1)}, bf16[16,1024,128]{2,1,0:T(8,128)(2,1)}, u32[]{:S(2)}) copy-start(bf16[16,1024,128]{2,1,0:T(8,128)(2,1)} %top.1) | copy-start | bytes 12582916
  43.3 0.8 %copy-start.1 = (bf16[2,128,128]{2,1,0:T(8,128)(2,1)S(1)}, bf16[2,128,128]{2,1,0:T(8,128)(2,1)}, u32[]{:S(2)}) copy-start(bf16[2,128,128]{2,1,0:T(8,128)(2,1)} %shard_map.82.coeff) | copy-start | bytes 196612

commit v3 on v2

--- a/solution.py
+++ b/solution.py
@@ -27,9 +27,8 @@
     return ring[(kb >> 1) & 3] + ring[z] + ring[ko & 3]
 
 
-PARTNERS = sorted(range(DEVICES), key=lambda k: (-hops(k), (k * 37) % DEVICES))
-PARTNERS.remove(0)
-PARTNERS.append(0)
+FARTHEST = sorted(range(1, DEVICES), key=lambda k: (-hops(k), (k * 37) % DEVICES))
+PARTNERS = FARTHEST[:14] + FARTHEST[:13:-1] + [0]
 
 
 ONE, ZERO = np.array(1, BF), np.array(0, BF)
@@ -78,7 +77,7 @@
         copy.start()
 
     barrier = pltpu.get_barrier_semaphore()
-    for k in PARTNERS[:-1]:
+    for k in FARTHEST:
         pl.semaphore_signal(
             barrier, inc=1, device_id=(b ^ (k // OWNERS), o ^ (k % OWNERS)), device_id_type=MESH
         )
@@ -300,17 +299,20 @@
             dma((LEVELS, GROUPS)),
         ],
         compiler_params=pltpu.CompilerParams(
-            collective_id=0, has_side_effects=True, vmem_limit_bytes=58 * 1024 * 1024
+            collective_id=0, has_side_effects=True, vmem_limit_bytes=50 * 1024 * 1024
         ),
-    )(
-        fourier,
-        cycle_lat.reshape(2 * DEVICES, 128),
-        order_table.reshape(1, ORDERS),
-        leaf_op,
-        level_op[:, 0],
-        skeleton.reshape(LEVELS * SLOTS, KR),
-        positions,
-    )
+    )(*(
+        pltpu.with_memory_space_constraint(x, pltpu.HBM)
+        for x in (
+            fourier,
+            cycle_lat.reshape(2 * DEVICES, 128),
+            order_table.reshape(1, ORDERS),
+            leaf_op,
+            level_op[:, 0],
+            skeleton.reshape(LEVELS * SLOTS, KR),
+            positions,
+        )
+    ))
     return pl.pallas_call(
         expand,
         out_shape=jax.ShapeDtypeStruct((COLS, SLOTS, LB), F32),

time: 46.5 us -> 42.6 us (0.916)
  Pallas kernels: 45.5 us -> 42.5 us
  local copies, waits for them, and re-layouts: 0.84 us -> 0.01 us
    pallas_call x1, Pallas kernels: 43.3 us -> 40.3 us  [per_device(): pl.pallas_call(analyse, out_shape=jax.ShapeDtypeStruct((GROUPS, WIDE, KR)...]
    unnamed x4 -> x2, local copies, waits for them, and re-layouts: 0.84 us -> 0.01 us
where the time goes in v3:
time: 42.6 us; the launch traced here: 42.5 us
  Pallas kernels  42.5 us (100%)
    pallas_call x1, Pallas kernels, per_device(): pl.pallas_call(analyse, out_shape=jax.ShapeDtypeStruct((GROUPS, WIDE, KR)...  40.3 us
    pallas_call x1, Pallas kernels, per_device(): pl.pallas_call(expand, out_shape=jax.ShapeDtypeStruct((COLS, SLOTS, LB),...  2.22 us

profile of v3, /device:TPU:0, one launch (start us, length us, event | category | flops | bytes accessed | tf_op | source)
XLA Modules:
  0.0 42.5 jit_solution(2716180346133222444)
XLA Ops:
  0.0 0.0 copy-start
  0.0 40.3 %shard_map.82.coeff = bf16[2,128,128]{2,1,0:T(8,128)(2,1)S(1)} custom-call(bf16[16,128,256]{2,1,0:T(8,128)(2,1)} %fourier.1, s32[256,128]{1,0:T(8,128)} %bitcast.5, s32[1,128]{1,0:T(1,128)} %bitcast.7, bf16[16,128,2048]{2,1,0:T(8,128)(2,1)} %leaf.1, bf16[4,16,128,256]{3,2,1,0:T(8,128)(2,1)} %bitcast.4, s32[64,128]{1,0:T(8,128)} %bitcast.6, ...), custom_call_target="tpu_custom_call" | custom-call | tf_op jit(solution)/shard_map/pallas_call | solution.py:272
  40.3 0.0 copy-done
  40.3 2.2 %shard_map.83 = f32[16,16,1024]{2,1,0:T(8,128)} custom-call(bf16[2,128,128]{2,1,0:T(8,128)(2,1)S(1)} %shard_map.82.coeff, bf16[16,1024,128]{2,1,0:T(8,128)(2,1)S(1)} %copy-done), custom_call_target="tpu_custom_call" | custom-call | tf_op jit(solution)/shard_map/pallas_call | solution.py:316
Async XLA Ops:
  0.0 40.3 %copy-start = (bf16[16,1024,128]{2,1,0:T(8,128)(2,1)S(1)}, bf16[16,1024,128]{2,1,0:T(8,128)(2,1)}, u32[]{:S(2)}) copy-start(bf16[16,1024,128]{2,1,0:T(8,128)(2,1)} %top.1) | copy-start | bytes 12582916

commit v4 on v3

--- a/solution.py
+++ b/solution.py
@@ -51,9 +51,9 @@
 
 
 def analyse(
-    fourier, lat, otab, leaf, level, skel, korder, out,
-    fv, latv, otabv, leafv, mixv, skelv, kordv,
-    wide, sendb, recvb, placing, turned, total, field, products, comb,
+    fourier, lat, otab, leaf, level, skel, korder, top, out, top_out,
+    topv, fv, latv, otabv, leafv, mixv, skelv, kordv,
+    wide, sendb, recvb, placing, turned, total, field, comb,
     in_sem, send_sem, recv_sem, own_sem, x_send, x_recv,
 ):
     b, o = lax.axis_index("blk"), lax.axis_index("order")
@@ -72,6 +72,7 @@
         pltpu.make_async_copy(
             level.at[:, :, :, pl.ds(KR, KR)], mixv.at[:, :, :, pl.ds(2 * KR, KR)], in_sem.at[7]
         ),
+        pltpu.make_async_copy(top, topv, in_sem.at[8]),
     ]
     for copy in loads[:3]:
         copy.start()
@@ -163,10 +164,10 @@
 
     lane_slot = iota((KR, WIDE), 1) & (HALF - 1)
 
-    def own_lanes(rows):
-        kept = rows[:KR]
+    def own_lanes(rows_of, x):
+        kept = dot(rows_of(0), x)
         for s in range(1, HALF):
-            kept = jnp.where(lane_slot == s, rows[s * KR:(s + 1) * KR], kept)
+            kept = jnp.where(lane_slot == s, dot(rows_of(s), x), kept)
         return kept
 
     def exchange(j, g, coeff):
@@ -177,9 +178,6 @@
         )
         copy.start()
         return copy
-
-    def slot_rows(ref, g):
-        return ref[g * HALF:(g + 1) * HALF].reshape(HALF * KR, ref.shape[2])
 
     def lanes_of(g):
         return slice(g * WIDE, (g + 1) * WIDE)
@@ -191,6 +189,14 @@
             turned[4 * i * KR:4 * (i + 1) * KR, n * TILE:(n + 1) * TILE] = dot(
                 some, placing[HEAD + n]
             ).astype(BF)
+
+    loads[8].wait()
+    eye = ones_where(iota((TILE, TILE), 0) == iota((TILE, TILE), 1)).astype(BF)
+    for pair in range(SLOTS // 2):
+        for i in range(LB // PART):
+            at = slice(i * PART, (i + 1) * PART)
+            both = jnp.concatenate([topv[2 * pair, at, :], topv[2 * pair + 1, at, :]], axis=1)
+            top_out[pair * 2 * KR:(pair + 1) * 2 * KR, at] = dot_nt(eye, both).astype(BF)
 
     def landed(n):
         rows = TILE if n < CHUNKS - 1 else TILE - RPB
@@ -208,14 +214,12 @@
             field[...] = (total[...] + moved).astype(BF)
     partial = []
     for g in range(GROUPS):
-        products[...] = dot(slot_rows(leafv, g), field[:, lanes_of(g)])
-        partial.append(own_lanes(products[...]))
+        partial.append(own_lanes(lambda s: leafv[g * HALF + s], field[:, lanes_of(g)]))
 
     def level_part(j, g, half):
         x = comb[j, g, half * KR:(half + 1) * KR, :]
-        rows = slot_rows(mixv.at[j], g)[:, 2 * half * KR:2 * (half + 1) * KR]
-        products[...] = dot(rows, jnp.concatenate([x, x], axis=0))
-        return own_lanes(products[...])
+        part = slice(2 * half * KR, 2 * (half + 1) * KR)
+        return own_lanes(lambda s: mixv[j, g * HALF + s, :, part], jnp.concatenate([x, x], axis=0))
 
     for n in range(HEAD, CHUNKS):
         landed(n)
@@ -223,9 +227,10 @@
     pltpu.make_async_copy(mine, mine, own_sem).wait()
     copies = [[None] * GROUPS for _ in range(LEVELS)]
     for g in range(GROUPS):
-        rows = turned[g * HALF * KR:(g + 1) * HALF * KR, :]
-        products[...] = dot(rows, recvb[HEAD * TILE:, lanes_of(g)])
-        copies[0][g] = exchange(0, g, partial[g] + own_lanes(products[...]))
+        rest = own_lanes(
+            lambda s: turned[(g * HALF + s) * KR:(g * HALF + s + 1) * KR, :], recvb[HEAD * TILE:, lanes_of(g)]
+        )
+        copies[0][g] = exchange(0, g, partial[g] + rest)
     loads[6].wait()
     loads[7].wait()
     for j in range(LEVELS):
@@ -256,8 +261,8 @@
     for n in range(LB // PART):
         at = pl.ds(n * PART, PART)
         for g in range(GROUPS):
-            wanted = jnp.concatenate([top[g * HALF + s, at, :] for s in range(HALF)], axis=1)
-            block[:, g * HALF:(g + 1) * HALF, at] = dot_nt(spread[g], wanted).reshape(COLS, HALF, PART)
+            wanted = top[g * HALF * KR:(g + 1) * HALF * KR, at]
+            block[:, g * HALF:(g + 1) * HALF, at] = dot(spread[g], wanted).reshape(COLS, HALF, PART)
         copy = pltpu.make_async_copy(block.at[:, :, at], out.at[:, :, at], sem.at[n])
         copy.start()
         stores.append(copy)
@@ -269,12 +274,16 @@
     positions = jnp.asarray(np.repeat(np.array(PARTNERS, np.int32), RPB).reshape(1, RB))
     hbm = pl.BlockSpec(memory_space=pltpu.HBM)
     dma = pltpu.SemaphoreType.DMA
-    coeff = pl.pallas_call(
+    coeff, top_turned = pl.pallas_call(
         analyse,
-        out_shape=jax.ShapeDtypeStruct((GROUPS, WIDE, KR), BF),
-        in_specs=[hbm] * 7,
-        out_specs=pl.BlockSpec(memory_space=pltpu.VMEM),
+        out_shape=(
+            jax.ShapeDtypeStruct((GROUPS, WIDE, KR), BF),
+            jax.ShapeDtypeStruct((SLOTS * KR, LB), BF),
+        ),
+        in_specs=[hbm] * 8,
+        out_specs=[pl.BlockSpec(memory_space=pltpu.VMEM)] * 2,
         scratch_shapes=[
+            pltpu.VMEM((SLOTS, LB, KR), BF),
             pltpu.VMEM((COLS, ORDERS, ROWS), BF),
             pltpu.VMEM((2 * DEVICES, 128), I32),
             pltpu.VMEM((1, ORDERS), I32),
@@ -289,9 +298,8 @@
             pltpu.VMEM((SLOTS * KR, TAIL * TILE), BF),
             pltpu.VMEM((RB, GROUPS * WIDE), F32),
             pltpu.VMEM((RB, GROUPS * WIDE), BF),
-            pltpu.VMEM((HALF * KR, WIDE), F32),
             pltpu.VMEM((LEVELS, GROUPS, 2 * KR, WIDE), BF),
-            dma((8,)),
+            dma((9,)),
             dma,
             dma((CHUNKS,)),
             dma,
@@ -299,7 +307,7 @@
             dma((LEVELS, GROUPS)),
         ],
         compiler_params=pltpu.CompilerParams(
-            collective_id=0, has_side_effects=True, vmem_limit_bytes=50 * 1024 * 1024
+            collective_id=0, has_side_effects=True, vmem_limit_bytes=44 * 1024 * 1024
         ),
     )(*(
         pltpu.with_memory_space_constraint(x, pltpu.HBM)
@@ -311,6 +319,7 @@
             level_op[:, 0],
             skeleton.reshape(LEVELS * SLOTS, KR),
             positions,
+            top_op,
         )
     ))
     return pl.pallas_call(
@@ -320,7 +329,7 @@
         out_specs=pl.BlockSpec(memory_space=pl.ANY),
         scratch_shapes=[pltpu.VMEM((COLS, SLOTS, LB), F32), dma((LB // PART,))],
         compiler_params=pltpu.CompilerParams(vmem_limit_bytes=16 * 1024 * 1024),
-    )(coeff, top_op)
+    )(coeff, top_turned)
 
 
 def solution(mesh):

time: 42.6 us -> 40.9 us (0.960)
  Pallas kernels: 42.5 us -> 40.6 us
    pallas_call x1, Pallas kernels: 40.3 us -> 39.2 us  [per_device(): pl.pallas_call(analyse, out_shape=(jax.ShapeDtypeStruct((GROUPS, WIDE, KR...]
    pallas_call x1, Pallas kernels: 2.22 us -> 1.48 us  [per_device(): pl.pallas_call(expand, out_shape=jax.ShapeDtypeStruct((COLS, SLOTS, LB),...]
where the time goes in v4:
time: 40.9 us; the launch traced here: 40.8 us
  Pallas kernels  40.6 us (99%)
    pallas_call x1, Pallas kernels, per_device(): pl.pallas_call(analyse, out_shape=(jax.ShapeDtypeStruct((GROUPS, WIDE, KR...  39.2 us
    pallas_call x1, Pallas kernels, per_device(): pl.pallas_call(expand, out_shape=jax.ShapeDtypeStruct((COLS, SLOTS, LB),...  1.48 us

profile of v4, /device:TPU:0, one launch (start us, length us, event | category | flops | bytes accessed | tf_op | source)
XLA Modules:
  0.0 40.8 jit_solution(218720337269539922)
XLA Ops:
  0.0 39.2 %shard_map.82 = (bf16[2,128,128]{2,1,0:T(8,128)(2,1)S(1)}, bf16[2048,1024]{1,0:T(8,128)(2,1)S(1)}) custom-call(bf16[16,128,256]{2,1,0:T(8,128)(2,1)} %fourier.1, s32[256,128]{1,0:T(8,128)} %bitcast.5, s32[1,128]{1,0:T(1,128)} %bitcast.7, bf16[16,128,2048]{2,1,0:T(8,128)(2,1)} %leaf.1, bf16[4,16,128,256]{3,2,1,0:T(8,128)(2,1)} %bitcast.4, s32[64,128]{1,0:T(8,128)} %bitcast.6, ...), custom_call_target="tpu_custom_call" | custom-call | tf_op jit(solution)/shard_map/pallas_call | solution.py:277
  39.2 1.5 %shard_map.83 = f32[16,16,1024]{2,1,0:T(8,128)} custom-call(bf16[2,128,128]{2,1,0:T(8,128)(2,1)S(1)} %get-tuple-element.7.coeff, bf16[2048,1024]{1,0:T(8,128)(2,1)S(1)} %get-tuple-element.8.top), custom_call_target="tpu_custom_call" | custom-call | tf_op jit(solution)/shard_map/pallas_call | solution.py:325

commit v5 on v4

--- a/solution.py
+++ b/solution.py
@@ -225,7 +225,7 @@
         landed(n)
     mine = recvb.at[pl.ds(RB - RPB, RPB), :]
     pltpu.make_async_copy(mine, mine, own_sem).wait()
-    copies = [[None] * GROUPS for _ in range(LEVELS)]
+    copies, coeffs = [[None] * GROUPS for _ in range(LEVELS)], []
     for g in range(GROUPS):
         rest = own_lanes(
             lambda s: turned[(g * HALF + s) * KR:(g * HALF + s + 1) * KR, :], recvb[HEAD * TILE:, lanes_of(g)]
@@ -241,7 +241,9 @@
             if j + 1 < LEVELS:
                 copies[j + 1][g] = exchange(j + 1, g, coeff)
             else:
-                out[g] = jnp.transpose(coeff).astype(BF)
+                coeffs.append(coeff)
+    for g in range(GROUPS):
+        out[g] = jnp.transpose(coeffs[g]).astype(BF)
     for row in copies:
         for copy in row:
             copy.wait_send()

time: 40.9 us -> 40.9 us (level)
  no operation moved by 1% of the time
where the time goes in v5:
time: 40.9 us; the launch traced here: 40.8 us
  Pallas kernels  40.6 us (99%)
    pallas_call x1, Pallas kernels, per_device(): pl.pallas_call(analyse, out_shape=(jax.ShapeDtypeStruct((GROUPS, WIDE, KR...  39.2 us
    pallas_call x1, Pallas kernels, per_device(): pl.pallas_call(expand, out_shape=jax.ShapeDtypeStruct((COLS, SLOTS, LB),...  1.48 us

profile of v5, /device:TPU:0, one launch (start us, length us, event | category | flops | bytes accessed | tf_op | source)
XLA Modules:
  0.0 40.8 jit_solution(8893775745891037154)
XLA Ops:
  0.0 39.2 %shard_map.82 = (bf16[2,128,128]{2,1,0:T(8,128)(2,1)S(1)}, bf16[2048,1024]{1,0:T(8,128)(2,1)S(1)}) custom-call(bf16[16,128,256]{2,1,0:T(8,128)(2,1)} %fourier.1, s32[256,128]{1,0:T(8,128)} %bitcast.5, s32[1,128]{1,0:T(1,128)} %bitcast.7, bf16[16,128,2048]{2,1,0:T(8,128)(2,1)} %leaf.1, bf16[4,16,128,256]{3,2,1,0:T(8,128)(2,1)} %bitcast.4, s32[64,128]{1,0:T(8,128)} %bitcast.6, ...), custom_call_target="tpu_custom_call" | custom-call | tf_op jit(solution)/shard_map/pallas_call | solution.py:279
  39.2 1.5 %shard_map.83 = f32[16,16,1024]{2,1,0:T(8,128)} custom-call(bf16[2,128,128]{2,1,0:T(8,128)(2,1)S(1)} %get-tuple-element.7.coeff, bf16[2048,1024]{1,0:T(8,128)(2,1)S(1)} %get-tuple-element.8.top), custom_call_target="tpu_custom_call" | custom-call | tf_op jit(solution)/shard_map/pallas_call | solution.py:327
